TPU v7x, 32 devices: a whole 2x2x4 slice. The times are simulated.
32 devices in a mesh: groups: 2 (over y), row: 4 (over z), col: 2 (over x), rep: 2 (over core).
Axes of the slice: x: 2, y: 2, z: 4, core: 2. Of those that a mesh axis runs over, the one named last changes fastest.
Arguments:
- left_blocks: bfloat16 [8, 4, 12, 128, 128], P(('groups', 'row'), ('col', 'rep')), parts along dimension 0, may hold values from -4 to 4
- left_coords: int32 [8, 4, 2, 12], P(('groups', 'row'), ('col', 'rep')), parts along dimension 0, may hold values from -1 to 27, as said below
- right_blocks: bfloat16 [8, 4, 12, 128, 128], P(('groups', 'row'), ('col', 'rep')), parts along dimension 0, may hold values from -4 to 4
- right_coords: int32 [8, 4, 2, 12], P(('groups', 'row'), ('col', 'rep')), parts along dimension 0, may hold values from -1 to 27, as said below
Outputs:
- product: bfloat16 [8192, 4096], P(('groups', 'row'), ('col', 'rep')), parts along dimension 0
There are 2 independent parts, one for each index of `groups`. A program takes and returns all parts, laid end to end along the dimension named above; each array names one. Nothing has to cross between parts.
Inputs may be any that keep to these rules, and one draw needn't show every extreme that they name: `left_coords`: in every tile the live slots come first and hold distinct positions; slots after them have both coordinates -1. Every tile holds at least one live slot and at most 12, and some tile holds exactly 12. `right_coords`: in every tile the live slots come first and hold distinct positions; slots after them have both coordinates -1. Every tile holds at least two live slots and at most 12, some tile exactly 12; no block row of a tile holds more than 2 live slots, and in every tile some block row holds exactly 2.
All inputs are finite; a program needn't handle non-finite values.
Results may differ from a plain program's by a relative error of at most 0.001.
Values may be sent and summed in bfloat16 or wider, within the bound.
No kernel may reach another device: no remote copies, remote signals or barrier semaphores. Data moves between devices by JAX's collectives and lax.ppermute only.
A program may use at most 64 MiB of HBM per device.

v0:
```python
import jax
import jax.numpy as jnp
from jax import lax
from jax.sharding import PartitionSpec as P

BS = 128
RB = 8
WR = 2


def as_sent(shard):
    return jax.tree.map(lambda a: a.astype(jnp.bfloat16) if a.dtype == jnp.float32 else a, shard)


def from_behind(block, axis, distance):
    devices = range(lax.axis_size(axis))
    route = [((i - distance) % len(devices), i) for i in devices]
    return lax.ppermute(block, axis, route)


def add_terms(summed, left_vals, left_pos, right_vals, right_pos):
    slot_count = left_vals.shape[0]
    left_row = left_pos[0]
    left_col = left_pos[1]
    right_row = right_pos[0]
    right_col = right_pos[1]
    matches = (
        (left_col[:, None] == right_row[None, :])
        & (left_col[:, None] >= 0)
        & (right_row[None, :] >= 0)
    )
    ranking = jnp.cumsum(matches.astype(jnp.int32), axis=1)
    levels = jnp.arange(1, WR + 1, dtype=jnp.int32)
    chosen = (matches[:, None, :] & (ranking[:, None, :] == levels[None, :, None])).astype(
        jnp.int32
    )
    present = jnp.sum(chosen, axis=2)
    partner = jnp.sum(chosen * jnp.arange(slot_count, dtype=jnp.int32)[None, None, :], axis=2)
    picked = right_vals[partner]
    products = jnp.einsum("aij,awjk->awik", left_vals, picked, preferred_element_type=jnp.float32)
    target = left_row[:, None] * RB + right_col[partner]
    is_live = (present > 0) & (left_row[:, None] >= 0)
    masked = jnp.where(is_live[:, :, None, None], products, 0.0).reshape(slot_count * WR, BS * BS)
    places = jnp.where(is_live, target, 0).reshape(slot_count * WR).astype(jnp.int32)
    return summed.at[places].add(masked)


def skew_left(left_vals, left_pos, offset, bit_number):
    moved_vals, moved_pos = (
        from_behind(left_vals, ("col", "rep"), -(1 << bit_number)),
        from_behind(as_sent(left_pos), ("col", "rep"), -(1 << bit_number)).astype(left_pos.dtype),
    )
    selected = offset >> bit_number & 1 == 1
    return (jnp.where(selected, moved_vals, left_vals), jnp.where(selected, moved_pos, left_pos))


def skew_right(right_vals, right_pos, offset, bit_number):
    moved_vals, moved_pos = (
        from_behind(right_vals, "row", -(1 << bit_number)),
        from_behind(as_sent(right_pos), "row", -(1 << bit_number)).astype(right_pos.dtype),
    )
    selected = offset >> bit_number & 1 == 1
    return (jnp.where(selected, moved_vals, right_vals), jnp.where(selected, moved_pos, right_pos))


def per_device(left_blocks, left_coords, right_blocks, right_coords):
    grid_size = lax.axis_size("row")
    start_sum = jnp.zeros((RB * RB, BS * BS), jnp.float32)
    left_vals = left_blocks[0, 0]
    left_pos = left_coords[0, 0]
    right_vals = right_blocks[0, 0]
    right_pos = right_coords[0, 0]
    here_row = lax.axis_index("row")
    here_col = lax.axis_index(("col", "rep"))
    for bit_number in range((grid_size - 1).bit_length()):
        left_vals, left_pos = skew_left(left_vals, left_pos, here_row, bit_number)
        right_vals, right_pos = skew_right(right_vals, right_pos, here_col, bit_number)

    def advance(step_index, carried):
        summed, left_vals, left_pos, right_vals, right_pos = carried
        summed = add_terms(summed, left_vals, left_pos, right_vals, right_pos)
        left_vals, left_pos = (
            from_behind(left_vals, ("col", "rep"), -1),
            from_behind(as_sent(left_pos), ("col", "rep"), -1).astype(left_pos.dtype),
        )
        right_vals, right_pos = (
            from_behind(right_vals, "row", -1),
            from_behind(as_sent(right_pos), "row", -1).astype(right_pos.dtype),
        )
        return (summed, left_vals, left_pos, right_vals, right_pos)

    carried = lax.fori_loop(
        0, grid_size - 1, advance, (start_sum, left_vals, left_pos, right_vals, right_pos)
    )
    summed, left_vals, left_pos, right_vals, right_pos = carried
    summed = add_terms(summed, left_vals, left_pos, right_vals, right_pos)
    return (
        summed.reshape(RB, RB, BS, BS)
        .transpose(0, 2, 1, 3)
        .reshape(RB * BS, RB * BS)
        .astype(jnp.bfloat16)
    )


def solution(mesh):
    return jax.shard_map(
        per_device,
        mesh=mesh,
        in_specs=(
            P(("groups", "row"), ("col", "rep"), None, None, None),
            P(("groups", "row"), ("col", "rep"), None, None),
            P(("groups", "row"), ("col", "rep"), None, None, None),
            P(("groups", "row"), ("col", "rep"), None, None),
        ),
        out_specs=P(("groups", "row"), ("col", "rep")),
        check_vma=False,
    )
```

profile of v0, /device:TPU:0, one launch (start us, length us, event | category | flops | bytes accessed | tf_op | source)
XLA Modules:
  0.0 121.2 jit_solution(12854167672030480855)
XLA Ops:
  0.0 5.0 %collective-permute-start.8 = (bf16[12,128,128]{2,1,0:T(8,128)(2,1)}, bf16[12,128,128]{2,1,0:T(8,128)(2,1)S(1)}, u32[]{:S(2)}, u32[]{:S(2)}) collective-permute-start(bf16[12,128,128]{2,1,0:T(8,128)(2,1)} %bitcast.111), channel_id=1, source_target_pairs={{4,0},{8,4},{12,8},{0,12},{5,1},{9,5},{13,9},{1,13},{6,2},{10,6},{... | collective-permute-start | bytes 1179656 | tf_op jit(solution)/shard_map/ppermute | solution.py:18
  7.6 6.1 %collective-permute-done.10 = s32[2,12]{1,0:T(2,128)S(1)} collective-permute-done((s32[2,12]{1,0:T(2,128)}, s32[2,12]{1,0:T(2,128)S(1)}, u32[]{:S(2)}, u32[]{:S(2)}) %collective-permute-start.10) | collective-permute-done | bytes 128 | tf_op jit(solution)/shard_map/ppermute | solution.py:18
  16.5 1.5 %collective-permute-start.7 = (s32[2,12]{1,0:T(2,128)S(1)}, s32[2,12]{1,0:T(2,128)S(1)}, u32[]{:S(2)}, u32[]{:S(2)}) collective-permute-start(s32[2,12]{1,0:T(2,128)S(1)} %broadcast_select_fusion.6), channel_id=1, source_target_pairs={{2,0},{3,1},{0,2},{1,3},{6,4},{7,5},{4,6},{5,7},{10,8},{11,9},{8,1... | collective-permute-start | bytes 296 | tf_op jit(solution)/shard_map/ppermute | solution.py:18
  20.5 1.5 %collective-permute-start.9 = (bf16[12,128,128]{2,1,0:T(8,128)(2,1)S(1)}, bf16[12,128,128]{2,1,0:T(8,128)(2,1)S(1)}, u32[]{:S(2)}, u32[]{:S(2)}) collective-permute-start(bf16[12,128,128]{2,1,0:T(8,128)(2,1)S(1)} %broadcast_select_fusion), channel_id=1, source_target_pairs={{8,0},{12,4},{0,8},{4,12},{9,1},{13,5},{1,9},{5,13},{10,2},{14,6},... | collective-permute-start | bytes 1179656 | tf_op jit(solution)/shard_map/ppermute | solution.py:18
  23.0 1.6 %collective-permute-start.5 = (bf16[12,128,128]{2,1,0:T(8,128)(2,1)S(1)}, bf16[12,128,128]{2,1,0:T(8,128)(2,1)S(1)}, u32[]{:S(2)}, u32[]{:S(2)}) collective-permute-start(bf16[12,128,128]{2,1,0:T(8,128)(2,1)S(1)} %broadcast_select_fusion.2), channel_id=1, source_target_pairs={{2,0},{3,1},{0,2},{1,3},{6,4},{7,5},{4,6},{5,7},{10,8},{11,9},{8,1... | collective-permute-start | bytes 1179656 | tf_op jit(solution)/shard_map/ppermute | solution.py:18
  25.1 13.6 %collective-permute-done.9 = bf16[12,128,128]{2,1,0:T(8,128)(2,1)S(1)} collective-permute-done((bf16[12,128,128]{2,1,0:T(8,128)(2,1)S(1)}, bf16[12,128,128]{2,1,0:T(8,128)(2,1)S(1)}, u32[]{:S(2)}, u32[]{:S(2)}) %collective-permute-start.9) | collective-permute-done | bytes 393248 | tf_op jit(solution)/shard_map/ppermute | solution.py:18
  40.3 2.3 %broadcast_in_dim.33 = f32[64,16384]{1,0:T(8,128)} broadcast(f32[]{:T(128)} %constant.25.clone.1), dimensions={} | broadcast | bytes 4194308 | tf_op jit(solution)/shard_map/broadcast_in_dim | solution.py:68
  42.6 58.7 %while.18 = (s32[]{:T(128)}, f32[64,16384]{1,0:T(8,128)}, bf16[12,128,128]{2,1,0:T(8,128)(2,1)}, s32[2,12]{1,0:T(2,128)}, bf16[12,128,128]{2,1,0:T(8,128)(2,1)}, /*index=5*/s32[2,12]{1,0:T(2,128)}, s32[]{:T(128)}, s32[]{:T(128)}) while((s32[]{:T(128)}, f32[64,16384]{1,0:T(8,128)}, bf16[12,128,128]{2,1,0:T(8,128)(2,1)}, s32[2,12]{1,0:T(2,128)}, ...), condition=%wide.region_5.6_spmd, body=%wide.region_0.5_spmd.sunk | while | flops 101454880 | bytes 17968064 | solution.py:92
  43.9 3.4 %collective-permute-start.3 = (s32[2,12]{1,0:T(2,128)S(1)}, s32[2,12]{1,0:T(2,128)}, u32[]{:S(2)}, u32[]{:S(2)}) collective-permute-start(s32[2,12]{1,0:T(2,128)S(1)} %copy.60), channel_id=1, source_target_pairs={{4,0},{8,4},{12,8},{0,12},{5,1},{9,5},{13,9},{1,13},{6,2},{10,6},{... | collective-permute-start | bytes 296 | tf_op jit(solution)/shard_map/while/body/eval_jaxpr/ppermute | solution.py:18
  47.3 1.8 %copy.57 = bf16[12,128,128]{2,1,0:T(8,128)(2,1)} copy(bf16[12,128,128]{2,1,0:T(8,128)(2,1)} %get-tuple-element.157) | data formatting | bytes 786432 | tf_op jit(solution)/shard_map
  53.2 1.4 %select_bitcast_fusion.3 = f32[12,2,128,128]{2,3,1,0:T(8,128)S(1)} fusion(bf16[12,2,128,128]{3,2,1,0:T(8,128)(2,1)S(1)} %bitcast.107, pred[12,2]{1,0:T(8,128)(4,1)S(1)} %get-tuple-element.146, bf16[12,128,128]{2,1,0:T(8,128)(2,1)} %copy.57), kind=kOutput, calls=%fused_computation.9.clone.1 | convolution fusion | flops 101056512 | bytes 2752536 | tf_op jit(solution)/shard_map/while/body/eval_jaxpr/aij,awjk->awik/dot_general | solution.py:40
  55.2 7.3 %scatter_custom_fusion.7 = f32[64,16384]{1,0:T(8,128)} fusion(f32[64,16384]{1,0:T(8,128)} %get-tuple-element.156, s32[24]{0:T(128)S(1)} %fusion.33, f32[3,8,128,128]{3,2,1,0:T(8,128)S(1)} %bitcast.106), kind=kCustom, calls=%fused_computation.6.clone.1 | custom fusion | flops 393216 | bytes 5767168 | tf_op jit(solution)/shard_map/while/body/eval_jaxpr/scatter-add | solution.py:45
  65.1 1.8 %copy.57 = bf16[12,128,128]{2,1,0:T(8,128)(2,1)} copy(bf16[12,128,128]{2,1,0:T(8,128)(2,1)} %get-tuple-element.157) | data formatting | bytes 786432 | tf_op jit(solution)/shard_map
  72.1 1.4 %select_bitcast_fusion.3 = f32[12,2,128,128]{2,3,1,0:T(8,128)S(1)} fusion(bf16[12,2,128,128]{3,2,1,0:T(8,128)(2,1)S(1)} %bitcast.107, pred[12,2]{1,0:T(8,128)(4,1)S(1)} %get-tuple-element.146, bf16[12,128,128]{2,1,0:T(8,128)(2,1)} %copy.57), kind=kOutput, calls=%fused_computation.9.clone.1 | convolution fusion | flops 101056512 | bytes 2752536 | tf_op jit(solution)/shard_map/while/body/eval_jaxpr/aij,awjk->awik/dot_general | solution.py:40
  74.1 7.3 %scatter_custom_fusion.7 = f32[64,16384]{1,0:T(8,128)} fusion(f32[64,16384]{1,0:T(8,128)} %get-tuple-element.156, s32[24]{0:T(128)S(1)} %fusion.33, f32[3,8,128,128]{3,2,1,0:T(8,128)S(1)} %bitcast.106), kind=kCustom, calls=%fused_computation.6.clone.1 | custom fusion | flops 393216 | bytes 5767168 | tf_op jit(solution)/shard_map/while/body/eval_jaxpr/scatter-add | solution.py:45
  82.7 3.4 %collective-permute-start.3 = (s32[2,12]{1,0:T(2,128)S(1)}, s32[2,12]{1,0:T(2,128)}, u32[]{:S(2)}, u32[]{:S(2)}) collective-permute-start(s32[2,12]{1,0:T(2,128)S(1)} %copy.60), channel_id=1, source_target_pairs={{4,0},{8,4},{12,8},{0,12},{5,1},{9,5},{13,9},{1,13},{6,2},{10,6},{... | collective-permute-start | bytes 296 | tf_op jit(solution)/shard_map/while/body/eval_jaxpr/ppermute | solution.py:18
  86.0 1.8 %copy.57 = bf16[12,128,128]{2,1,0:T(8,128)(2,1)} copy(bf16[12,128,128]{2,1,0:T(8,128)(2,1)} %get-tuple-element.157) | data formatting | bytes 786432 | tf_op jit(solution)/shard_map
  92.0 1.4 %select_bitcast_fusion.3 = f32[12,2,128,128]{2,3,1,0:T(8,128)S(1)} fusion(bf16[12,2,128,128]{3,2,1,0:T(8,128)(2,1)S(1)} %bitcast.107, pred[12,2]{1,0:T(8,128)(4,1)S(1)} %get-tuple-element.146, bf16[12,128,128]{2,1,0:T(8,128)(2,1)} %copy.57), kind=kOutput, calls=%fused_computation.9.clone.1 | convolution fusion | flops 101056512 | bytes 2752536 | tf_op jit(solution)/shard_map/while/body/eval_jaxpr/aij,awjk->awik/dot_general | solution.py:40
  94.0 7.3 %scatter_custom_fusion.7 = f32[64,16384]{1,0:T(8,128)} fusion(f32[64,16384]{1,0:T(8,128)} %get-tuple-element.156, s32[24]{0:T(128)S(1)} %fusion.33, f32[3,8,128,128]{3,2,1,0:T(8,128)S(1)} %bitcast.106), kind=kCustom, calls=%fused_computation.6.clone.1 | custom fusion | flops 393216 | bytes 5767168 | tf_op jit(solution)/shard_map/while/body/eval_jaxpr/scatter-add | solution.py:45
  105.0 1.7 %gather_fusion.3 = bf16[24,128,128]{2,1,0:T(8,128)(2,1)S(1)} fusion(bf16[12,128,128]{2,1,0:T(8,128)(2,1)} %get-tuple-element.44, s32[1024]{0:T(1024)S(1)} %pad_clamp_fusion.1), kind=kCustom, calls=%fused_computation.3 | custom fusion | bytes 1572960 | tf_op jit(solution)/shard_map/gather | solution.py:39
  107.6 1.4 %select_bitcast_fusion.1 = f32[12,2,128,128]{2,3,1,0:T(8,128)S(1)} fusion(bf16[12,2,128,128]{3,2,1,0:T(8,128)(2,1)S(1)} %bitcast.110, pred[12,2]{1,0:T(8,128)(4,1)S(1)} %get-tuple-element.65, bf16[12,128,128]{2,1,0:T(8,128)(2,1)} %get-tuple-element.45), kind=kOutput, calls=%fused_computation.36 | convolution fusion | flops 101056512 | bytes 2752536 | tf_op jit(solution)/shard_map/aij,awjk->awik/dot_general | solution.py:40
  109.6 7.3 %scatter_custom_fusion.1 = f32[64,16384]{1,0:T(8,128)} fusion(f32[64,16384]{1,0:T(8,128)} %get-tuple-element.41, s32[24]{0:T(128)S(1)} %fusion.18, f32[3,8,128,128]{3,2,1,0:T(8,128)S(1)} %bitcast.109), kind=kCustom, calls=%fused_computation.33 | custom fusion | flops 393216 | bytes 5767168 | tf_op jit(solution)/shard_map/scatter-add | solution.py:45
  116.9 2.4 %convert_element_type.34 = bf16[64,16384]{1,0:T(8,128)(2,1)S(1)} convert(f32[64,16384]{1,0:T(8,128)} %scatter_custom_fusion.1) | non-fusion elementwise | flops 1048576 | bytes 6291456 | tf_op jit(solution)/shard_map/convert_element_type | solution.py:101
  119.3 1.9 %copy.39 = bf16[128,8,8,128]{3,1,2,0:T(8,128)(2,1)} copy(bf16[128,8,8,128]{3,2,1,0:T(8,128)(2,1)S(1)} %bitcast.108) | data formatting | bytes 4194304
  (124 shorter events, 36.4 us)
Async XLA Ops:
  0.0 19.5 %collective-permute-start.8 = (bf16[12,128,128]{2,1,0:T(8,128)(2,1)}, bf16[12,128,128]{2,1,0:T(8,128)(2,1)S(1)}, u32[]{:S(2)}, u32[]{:S(2)}) collective-permute-start(bf16[12,128,128]{2,1,0:T(8,128)(2,1)} %bitcast.111), channel_id=1, source_target_pairs={{4,0},{8,4},{12,8},{0,12},{5,1},{9,5},{13,9},{1,13},{6,2},{10,6},{... | collective-permute-start | bytes 1179656 | tf_op jit(solution)/shard_map/ppermute | solution.py:18
  5.0 8.7 %collective-permute-start.10 = (s32[2,12]{1,0:T(2,128)}, s32[2,12]{1,0:T(2,128)S(1)}, u32[]{:S(2)}, u32[]{:S(2)}) collective-permute-start(s32[2,12]{1,0:T(2,128)} %bitcast.113), channel_id=1, source_target_pairs={{4,0},{8,4},{12,8},{0,12},{5,1},{9,5},{13,9},{1,13},{6,2},{10,6},{... | collective-permute-start | bytes 296 | tf_op jit(solution)/shard_map/ppermute | solution.py:18
  5.5 16.5 %collective-permute-start.4 = (bf16[12,128,128]{2,1,0:T(8,128)(2,1)}, bf16[12,128,128]{2,1,0:T(8,128)(2,1)S(1)}, u32[]{:S(2)}, u32[]{:S(2)}) collective-permute-start(bf16[12,128,128]{2,1,0:T(8,128)(2,1)} %bitcast.112), channel_id=1, source_target_pairs={{1,0},{2,1},{3,2},{0,3},{5,4},{6,5},{7,6},{4,7},{9,8},{10,9},{11,1... | collective-permute-start | bytes 1179656 | tf_op jit(solution)/shard_map/ppermute | solution.py:18
  5.9 10.0 %collective-permute-start.6 = (s32[2,12]{1,0:T(2,128)}, s32[2,12]{1,0:T(2,128)S(1)}, u32[]{:S(2)}, u32[]{:S(2)}) collective-permute-start(s32[2,12]{1,0:T(2,128)} %bitcast.114), channel_id=1, source_target_pairs={{1,0},{2,1},{3,2},{0,3},{5,4},{6,5},{7,6},{4,7},{9,8},{10,9},{11,1... | collective-permute-start | bytes 296 | tf_op jit(solution)/shard_map/ppermute | solution.py:18
  14.4 4.5 %collective-permute-start.11 = (s32[2,12]{1,0:T(2,128)S(1)}, s32[2,12]{1,0:T(2,128)S(1)}, u32[]{:S(2)}, u32[]{:S(2)}) collective-permute-start(s32[2,12]{1,0:T(2,128)S(1)} %broadcast_select_fusion.4), channel_id=1, source_target_pairs={{8,0},{12,4},{0,8},{4,12},{9,1},{13,5},{1,9},{5,13},{10,2},{14,6},... | collective-permute-start | bytes 296 | tf_op jit(solution)/shard_map/ppermute | solution.py:18
  16.5 8.1 %collective-permute-start.7 = (s32[2,12]{1,0:T(2,128)S(1)}, s32[2,12]{1,0:T(2,128)S(1)}, u32[]{:S(2)}, u32[]{:S(2)}) collective-permute-start(s32[2,12]{1,0:T(2,128)S(1)} %broadcast_select_fusion.6), channel_id=1, source_target_pairs={{2,0},{3,1},{0,2},{1,3},{6,4},{7,5},{4,6},{5,7},{10,8},{11,9},{8,1... | collective-permute-start | bytes 296 | tf_op jit(solution)/shard_map/ppermute | solution.py:18
  20.5 18.2 %collective-permute-start.9 = (bf16[12,128,128]{2,1,0:T(8,128)(2,1)S(1)}, bf16[12,128,128]{2,1,0:T(8,128)(2,1)S(1)}, u32[]{:S(2)}, u32[]{:S(2)}) collective-permute-start(bf16[12,128,128]{2,1,0:T(8,128)(2,1)S(1)} %broadcast_select_fusion), channel_id=1, source_target_pairs={{8,0},{12,4},{0,8},{4,12},{9,1},{13,5},{1,9},{5,13},{10,2},{14,6},... | collective-permute-start | bytes 1179656 | tf_op jit(solution)/shard_map/ppermute | solution.py:18
  23.0 16.5 %collective-permute-start.5 = (bf16[12,128,128]{2,1,0:T(8,128)(2,1)S(1)}, bf16[12,128,128]{2,1,0:T(8,128)(2,1)S(1)}, u32[]{:S(2)}, u32[]{:S(2)}) collective-permute-start(bf16[12,128,128]{2,1,0:T(8,128)(2,1)S(1)} %broadcast_select_fusion.2), channel_id=1, source_target_pairs={{2,0},{3,1},{0,2},{1,3},{6,4},{7,5},{4,6},{5,7},{10,8},{11,9},{8,1... | collective-permute-start | bytes 1179656 | tf_op jit(solution)/shard_map/ppermute | solution.py:18
  43.2 19.3 %collective-permute-start.1 = (s32[2,12]{1,0:T(2,128)S(1)}, s32[2,12]{1,0:T(2,128)}, u32[]{:S(2)}, u32[]{:S(2)}) collective-permute-start(s32[2,12]{1,0:T(2,128)S(1)} %copy.58), channel_id=1, source_target_pairs={{1,0},{2,1},{3,2},{0,3},{5,4},{6,5},{7,6},{4,7},{9,8},{10,9},{11,1... | collective-permute-start | bytes 296 | tf_op jit(solution)/shard_map/while/body/eval_jaxpr/ppermute | solution.py:18
  43.9 18.6 %collective-permute-start.3 = (s32[2,12]{1,0:T(2,128)S(1)}, s32[2,12]{1,0:T(2,128)}, u32[]{:S(2)}, u32[]{:S(2)}) collective-permute-start(s32[2,12]{1,0:T(2,128)S(1)} %copy.60), channel_id=1, source_target_pairs={{4,0},{8,4},{12,8},{0,12},{5,1},{9,5},{13,9},{1,13},{6,2},{10,6},{... | collective-permute-start | bytes 296 | tf_op jit(solution)/shard_map/while/body/eval_jaxpr/ppermute | solution.py:18
  49.0 13.5 %collective-permute-start = (bf16[12,128,128]{2,1,0:T(8,128)(2,1)}, bf16[12,128,128]{2,1,0:T(8,128)(2,1)}, u32[]{:S(2)}, u32[]{:S(2)}) collective-permute-start(bf16[12,128,128]{2,1,0:T(8,128)(2,1)} %copy.57), channel_id=1, source_target_pairs={{1,0},{2,1},{3,2},{0,3},{5,4},{6,5},{7,6},{4,7},{9,8},{10,9},{11,1... | collective-permute-start | bytes 1179656 | tf_op jit(solution)/shard_map/while/body/eval_jaxpr/ppermute | solution.py:18
  50.3 12.3 %collective-permute-start.2 = (bf16[12,128,128]{2,1,0:T(8,128)(2,1)S(1)}, bf16[12,128,128]{2,1,0:T(8,128)(2,1)}, u32[]{:S(2)}, u32[]{:S(2)}) collective-permute-start(bf16[12,128,128]{2,1,0:T(8,128)(2,1)S(1)} %copy.59), channel_id=1, source_target_pairs={{4,0},{8,4},{12,8},{0,12},{5,1},{9,5},{13,9},{1,13},{6,2},{10,6},{... | collective-permute-start | bytes 1179656 | tf_op jit(solution)/shard_map/while/body/eval_jaxpr/ppermute | solution.py:18
  63.2 18.2 %collective-permute-start.1 = (s32[2,12]{1,0:T(2,128)S(1)}, s32[2,12]{1,0:T(2,128)}, u32[]{:S(2)}, u32[]{:S(2)}) collective-permute-start(s32[2,12]{1,0:T(2,128)S(1)} %copy.58), channel_id=1, source_target_pairs={{1,0},{2,1},{3,2},{0,3},{5,4},{6,5},{7,6},{4,7},{9,8},{10,9},{11,1... | collective-permute-start | bytes 296 | tf_op jit(solution)/shard_map/while/body/eval_jaxpr/ppermute | solution.py:18
  64.0 17.3 %collective-permute-start.3 = (s32[2,12]{1,0:T(2,128)S(1)}, s32[2,12]{1,0:T(2,128)}, u32[]{:S(2)}, u32[]{:S(2)}) collective-permute-start(s32[2,12]{1,0:T(2,128)S(1)} %copy.60), channel_id=1, source_target_pairs={{4,0},{8,4},{12,8},{0,12},{5,1},{9,5},{13,9},{1,13},{6,2},{10,6},{... | collective-permute-start | bytes 296 | tf_op jit(solution)/shard_map/while/body/eval_jaxpr/ppermute | solution.py:18
  66.8 14.5 %collective-permute-start = (bf16[12,128,128]{2,1,0:T(8,128)(2,1)}, bf16[12,128,128]{2,1,0:T(8,128)(2,1)}, u32[]{:S(2)}, u32[]{:S(2)}) collective-permute-start(bf16[12,128,128]{2,1,0:T(8,128)(2,1)} %copy.57), channel_id=1, source_target_pairs={{1,0},{2,1},{3,2},{0,3},{5,4},{6,5},{7,6},{4,7},{9,8},{10,9},{11,1... | collective-permute-start | bytes 1179656 | tf_op jit(solution)/shard_map/while/body/eval_jaxpr/ppermute | solution.py:18
  68.2 13.2 %collective-permute-start.2 = (bf16[12,128,128]{2,1,0:T(8,128)(2,1)S(1)}, bf16[12,128,128]{2,1,0:T(8,128)(2,1)}, u32[]{:S(2)}, u32[]{:S(2)}) collective-permute-start(bf16[12,128,128]{2,1,0:T(8,128)(2,1)S(1)} %copy.59), channel_id=1, source_target_pairs={{4,0},{8,4},{12,8},{0,12},{5,1},{9,5},{13,9},{1,13},{6,2},{10,6},{... | collective-permute-start | bytes 1179656 | tf_op jit(solution)/shard_map/while/body/eval_jaxpr/ppermute | solution.py:18
  82.0 19.3 %collective-permute-start.1 = (s32[2,12]{1,0:T(2,128)S(1)}, s32[2,12]{1,0:T(2,128)}, u32[]{:S(2)}, u32[]{:S(2)}) collective-permute-start(s32[2,12]{1,0:T(2,128)S(1)} %copy.58), channel_id=1, source_target_pairs={{1,0},{2,1},{3,2},{0,3},{5,4},{6,5},{7,6},{4,7},{9,8},{10,9},{11,1... | collective-permute-start | bytes 296 | tf_op jit(solution)/shard_map/while/body/eval_jaxpr/ppermute | solution.py:18
  82.7 18.6 %collective-permute-start.3 = (s32[2,12]{1,0:T(2,128)S(1)}, s32[2,12]{1,0:T(2,128)}, u32[]{:S(2)}, u32[]{:S(2)}) collective-permute-start(s32[2,12]{1,0:T(2,128)S(1)} %copy.60), channel_id=1, source_target_pairs={{4,0},{8,4},{12,8},{0,12},{5,1},{9,5},{13,9},{1,13},{6,2},{10,6},{... | collective-permute-start | bytes 296 | tf_op jit(solution)/shard_map/while/body/eval_jaxpr/ppermute | solution.py:18
  87.8 13.5 %collective-permute-start = (bf16[12,128,128]{2,1,0:T(8,128)(2,1)}, bf16[12,128,128]{2,1,0:T(8,128)(2,1)}, u32[]{:S(2)}, u32[]{:S(2)}) collective-permute-start(bf16[12,128,128]{2,1,0:T(8,128)(2,1)} %copy.57), channel_id=1, source_target_pairs={{1,0},{2,1},{3,2},{0,3},{5,4},{6,5},{7,6},{4,7},{9,8},{10,9},{11,1... | collective-permute-start | bytes 1179656 | tf_op jit(solution)/shard_map/while/body/eval_jaxpr/ppermute | solution.py:18
  89.0 12.3 %collective-permute-start.2 = (bf16[12,128,128]{2,1,0:T(8,128)(2,1)S(1)}, bf16[12,128,128]{2,1,0:T(8,128)(2,1)}, u32[]{:S(2)}, u32[]{:S(2)}) collective-permute-start(bf16[12,128,128]{2,1,0:T(8,128)(2,1)S(1)} %copy.59), channel_id=1, source_target_pairs={{4,0},{8,4},{12,8},{0,12},{5,1},{9,5},{13,9},{1,13},{6,2},{10,6},{... | collective-permute-start | bytes 1179656 | tf_op jit(solution)/shard_map/while/body/eval_jaxpr/ppermute | solution.py:18
where the time goes:
time: 122 us; the launch traced here: 121 us
  other arithmetic  44.4 us (36%)
  local copies, waits for them, and re-layouts  26.5 us (22%)
  starting transfers between devices  23.6 us (19%)
  waiting for transfers between devices  20.6 us (17%)
  matrix products  5.67 us (5%)
    scatter-add x4, other arithmetic, add_terms(): return summed.at[places].add(masked)  29.1 us
    ppermute x20, starting transfers between devices, from_behind(): return lax.ppermute(block, axis, route)  23.6 us
    ppermute x20, waiting for transfers between devices, from_behind(): return lax.ppermute(block, axis, route)  20.6 us
    another operation x12, local copies, waits for them, and re-layouts  12.2 us
    dot_general x4, matrix products, add_terms(): jnp.einsum('aij,awjk->awik', left_vals, picked, preferred_element_type=jn...  5.67 us
    gather x4, local copies, waits for them, and re-layouts, add_terms(): picked = right_vals[partner]  3.79 us
    gather x8, local copies, waits for them, and re-layouts, add_terms(): target = left_row[:, None] * RB + right_col[partner]  3.11 us
    reduce_sum x4, other arithmetic, add_terms(): jnp.sum(chosen * jnp.arange(slot_count, dtype=jnp.int32)[None, None, :],...  2.79 us
  transfers between devices with their start and end apart: 20, of which 3 were waited for; matrix products, arithmetic and copies ran while one was open for 43% of the time, Pallas kernels for 0%

commit v1 on v0

v1 whole, which is shorter than its diff:
```python
import functools

import jax
import jax.numpy as jnp
from jax import lax
from jax.experimental import pallas as pl
from jax.experimental.pallas import tpu as pltpu
from jax.sharding import PartitionSpec as P

BS = 128
RB = 8
KB = 28
TAIL = 16
CR = ("col", "rep")
HBM = pl.BlockSpec(memory_space=pltpu.HBM)
VMEM = pl.BlockSpec(memory_space=pltpu.VMEM)
SMEM = pl.BlockSpec(memory_space=pltpu.SMEM)


def kept(memory, *arrays):
    return [pltpu.with_memory_space_constraint(array, memory) for array in arrays]


def pack_kernel(right, right_pos, left, left_pos, right_out, left_out, pos, sems):
    rows, slots = right.shape[0], right_pos.shape[1]
    copies = [
        pltpu.make_async_copy(right, right_out.at[pl.ds(0, rows)], sems.at[0]),
        pltpu.make_async_copy(left, left_out.at[pl.ds(0, rows)], sems.at[1]),
        pltpu.make_async_copy(right_pos, pos.at[0], sems.at[2]),
        pltpu.make_async_copy(left_pos, pos.at[1], sems.at[3]),
    ]
    for copy in copies:
        copy.start()
    for i, packed in enumerate((right_out, left_out)):
        copies[2 + i].wait()
        tail = jnp.pad(pos[i].astype(jnp.float32), ((0, TAIL - 2), (0, BS - slots)))
        packed[pl.ds(rows, TAIL), :] = tail.astype(jnp.bfloat16)
    for copy in copies[:2]:
        copy.wait()


def pack(right, right_pos, left, left_pos):
    packed = pltpu.VMEM((right.shape[0] + TAIL, BS), jnp.bfloat16)
    return pl.pallas_call(
        pack_kernel,
        out_shape=(packed, packed),
        in_specs=[HBM] * 4,
        out_specs=(VMEM, VMEM),
        scratch_shapes=[
            pltpu.VMEM((2, *right_pos.shape), jnp.int32),
            pltpu.SemaphoreType.DMA((4,)),
        ],
        compiler_params=pltpu.CompilerParams(vmem_limit_bytes=4 * 2**20),
    )(*kept(pltpu.HBM, right, right_pos, left, left_pos))


def block(ref, i):
    return ref[pl.ds(pl.multiple_of(i * BS, BS), BS), :]


def read_tail(ref, rows, whole, i):
    whole[pl.ds(8 * i, 8), :] = ref[pl.ds(rows, TAIL), :][:8].astype(jnp.float32).astype(jnp.int32)


def find_pairs(lc, lp, rc, rp, slots, tab, pairs, count):
    for u in range(slots):
        at = rc[rp, u] + 1
        tab[at] = tab[at] * 32 + (u + 1)
    tab[0] = 0
    for s in range(slots):
        met = tab[lc[lp + 1, s] + 1]
        for which in (met & 31, met >> 5):
            u = jnp.maximum(which - 1, 0)
            place = jnp.maximum(lc[lp, s] * RB + rc[rp + 1, u], 0)
            pairs[count] = ((lp // 8 * slots + s) * slots + u) * 64 + place
            count = count + jnp.minimum(which, 1)
    for u in range(slots):
        tab[rc[rp, u] + 1] = 0
    return count


def add_pairs(pairs, start, end, lall, right, slots, acc, seen, touched, sent):
    def multiply(p, sent):
        pair = pairs[p]
        place = pair & 63
        slot = pair >> 6
        acc[pl.ds(pl.multiple_of(place * BS, BS), BS), :] += jnp.dot(
            block(lall, slot // slots), block(right, slot % slots), preferred_element_type=jnp.float32
        )
        touched[sent] = place
        first = 1 - seen[place]
        seen[place] = 1
        return sent + first

    return lax.fori_loop(start, end, multiply, sent)


def send_blocks(touched, sent, acc, stage, out, sem):
    def block_out(i, place):
        at = (
            pl.ds(pl.multiple_of((place >> 3) * BS, BS), BS),
            pl.ds(pl.multiple_of((place & 7) * BS, BS), BS),
        )
        return pltpu.make_async_copy(stage.at[i], out.at[at], sem)

    def send(i, carry):
        stage[i] = block(acc, touched[i]).astype(jnp.bfloat16)
        block_out(i, touched[i]).start()
        return carry

    def settle(i, carry):
        block_out(0, 0).wait()
        return carry

    lax.fori_loop(0, sent, send, 0)
    lax.fori_loop(0, sent, settle, 0)


def clear_scalars(*refs):
    for ref in refs:
        for i in range(ref.shape[0]):
            ref[i] = 0


def early_kernel(tiles, slots, links, *refs):
    lefts, rights = refs[:tiles], refs[tiles:-13]
    out, acc, lall, lc = refs[-13:-9]
    stage, zeros, whole, coords, tab, pairs, seen, touched, sems = refs[-9:]
    rows = slots * BS

    zeros[...] = jnp.zeros_like(zeros)
    clears = [
        pltpu.make_async_copy(zeros, out.at[pl.ds(i * BS, BS), :], sems.at[0]) for i in range(RB)
    ]
    for clear in clears:
        clear.start()
    for i, ref in enumerate(lefts):
        read_tail(ref, rows, whole, i)
    for b, ref in enumerate(rights):
        read_tail(ref, rows, whole, tiles + b)
    scalars = [
        pltpu.make_async_copy(whole.at[pl.ds(0, 8 * tiles)], lc, sems.at[1]),
        pltpu.make_async_copy(whole.at[pl.ds(8 * tiles, 8 * len(rights))], coords, sems.at[2]),
    ]
    for copy in scalars:
        copy.start()
    clear_scalars(tab, seen)
    for j, ref in enumerate(lefts):
        lall[pl.ds(j * rows, rows), :] = ref[pl.ds(0, rows), :]
    acc[...] = jnp.zeros_like(acc)
    for copy in scalars:
        copy.wait()

    sent = jnp.int32(0)
    for b, ref in enumerate(rights):
        count = find_pairs(lc, 8 * links[b], coords, 8 * b, slots, tab, pairs, jnp.int32(0))
        sent = add_pairs(pairs, 0, count, lall, ref, slots, acc, seen, touched, sent)
    for clear in clears:
        clear.wait()
    send_blocks(touched, sent, acc, stage, out, sems.at[3])


def late_kernel(options, slots, links, late, lc, lall, acc, *refs):
    rights = refs[: sum(options)]
    out, acc_out, stage, whole, coords, tab, pairs, seen, touched, sems = refs[sum(options) + 1 :]
    rows = slots * BS
    groups = []
    for option in options:
        groups.append(rights[:option])
        rights = rights[option:]

    def chosen(group, act):
        if len(group) == 1:
            act(group[0])
        else:
            for choice, ref in enumerate(group):
                pl.when(late[0] == choice)(functools.partial(act, ref))

    for b, group in enumerate(groups):
        chosen(group, lambda ref, b=b: read_tail(ref, rows, whole, b))
    scalars = pltpu.make_async_copy(whole, coords, sems.at[0])
    scalars.start()
    clear_scalars(tab, seen)
    scalars.wait()
    ends = [jnp.int32(0)]
    early = links.shape[0] - len(groups)
    for b in range(len(groups)):
        ends.append(
            find_pairs(lc, 8 * links[early + b], coords, 8 * b, slots, tab, pairs, ends[-1])
        )
    sent = jnp.int32(0)
    for b, group in enumerate(groups):
        for choice, ref in enumerate(group):
            end = ends[b + 1]
            if len(group) > 1:
                end = jnp.where(late[0] == choice, end, ends[b])
            sent = add_pairs(
                pairs, ends[b], end, lall, ref, slots, acc_out, seen, touched, sent
            )
    send_blocks(touched, sent, acc_out, stage, out, sems.at[1])


def multiply_tiles(links, late, lefts, early, later):
    tiles = len(lefts)
    slots = lefts[0].shape[0] // BS
    rows = slots * BS
    product = pltpu.HBM((RB * BS, RB * BS), jnp.bfloat16)
    sums = pltpu.VMEM((RB * RB * BS, BS), jnp.float32)
    scalars = lambda size: pltpu.SMEM((size,), jnp.int32)
    lists = [scalars(KB + 1), scalars(2 * slots * tiles + 8), scalars(RB * RB), scalars(RB * RB + 8)]
    stage = pltpu.VMEM((RB * RB, BS, BS), jnp.bfloat16)
    params = pltpu.CompilerParams(vmem_limit_bytes=8 * 2**20)
    out, acc, lall, lc = pl.pallas_call(
        functools.partial(early_kernel, tiles, slots),
        out_shape=(
            product,
            sums,
            pltpu.VMEM((tiles * rows, BS), jnp.bfloat16),
            pltpu.SMEM((8 * tiles, BS), jnp.int32),
        ),
        in_specs=[SMEM] + [VMEM] * (tiles + len(early)),
        out_specs=(HBM, VMEM, VMEM, SMEM),
        scratch_shapes=[
            stage,
            pltpu.VMEM((BS, RB * BS), jnp.bfloat16),
            pltpu.VMEM((8 * (tiles + len(early)), BS), jnp.int32),
            pltpu.SMEM((8 * len(early), BS), jnp.int32),
            *lists,
            pltpu.SemaphoreType.DMA((4,)),
        ],
        compiler_params=params,
    )(links, *kept(pltpu.VMEM, *lefts, *early))
    options = [len(group) for group in later]
    later = sum(later, [])
    return pl.pallas_call(
        functools.partial(late_kernel, options, slots),
        out_shape=(product, sums),
        in_specs=[SMEM] * 3 + [VMEM] * (2 + len(later)) + [HBM],
        out_specs=(HBM, VMEM),
        scratch_shapes=[
            stage,
            pltpu.VMEM((8 * len(options), BS), jnp.int32),
            pltpu.SMEM((8 * len(options), BS), jnp.int32),
            *lists,
            pltpu.SemaphoreType.DMA((2,)),
        ],
        input_output_aliases={4: 1, 5 + len(later): 0},
        compiler_params=params,
    )(links, late, lc, *kept(pltpu.VMEM, lall, acc, *later), *kept(pltpu.HBM, out))[0]


def shifted(block, axis, distance):
    size = lax.axis_size(axis)
    return lax.ppermute(block, axis, [((i - distance) % size, i) for i in range(size)])


def any_grid(right, left):
    rows, cols = lax.axis_size("row"), lax.axis_size(CR)
    row, col = lax.axis_index("row"), lax.axis_index(CR)
    rights = [right] + [shifted(right, "row", d) for d in range(1, rows)]
    lefts = [left] + [shifted(left, CR, d) for d in range(1, cols)]
    held = (row - jnp.arange(rows)) % rows
    links = (col - held) % cols
    late = jnp.zeros((1,), jnp.int32)
    return links.astype(jnp.int32), late, lefts, rights[:1], [[tile] for tile in rights[1:]]


def line_of_four(right, left):
    row, col = lax.axis_index("row"), lax.axis_index(CR)

    def along(block, route):
        return lax.ppermute(block, "row", route)

    across, swap = [(i, i ^ 2) for i in range(4)], [(i, i ^ 1) for i in range(4)]
    from_far = along(right, [(0, 2), (3, 1)])
    from_mirror = along(right, [(1, 2), (2, 1), (0, 3), (3, 0)])
    from_pair = along(right, [(0, 1), (1, 0), (2, 3), (3, 2)])
    left_x = lax.ppermute(left, CR, across)
    left_c = lax.ppermute(left, CR, swap)
    left_xc = lax.ppermute(left_x, CR, swap)
    relayed = along(from_mirror, [(1, 0), (2, 3)])

    held = jnp.stack([row, 3 - row, row ^ 2, row ^ 1])
    links = held ^ col
    late = jnp.where((row == 0) | (row == 3), 1, 0).astype(jnp.int32).reshape(1)
    lefts = [left, left_c, left_x, left_xc]
    later = [[from_far, relayed], [from_pair]]
    return links.astype(jnp.int32), late, lefts, [right, from_mirror], later


def per_device(left_blocks, left_coords, right_blocks, right_coords):
    grid = (lax.axis_size("row"), lax.axis_size("col"), lax.axis_size("rep"))
    gather = line_of_four if grid == (4, 2, 2) else any_grid
    right, left = pack(
        right_blocks.reshape(-1, BS), right_coords[0, 0], left_blocks.reshape(-1, BS), left_coords[0, 0]
    )
    return multiply_tiles(*gather(right, left))


def solution(mesh):
    return jax.shard_map(
        per_device,
        mesh=mesh,
        in_specs=(
            P(("groups", "row"), CR, None, None, None),
            P(("groups", "row"), CR, None, None),
            P(("groups", "row"), CR, None, None, None),
            P(("groups", "row"), CR, None, None),
        ),
        out_specs=P(("groups", "row"), CR),
        check_vma=False,
    )
```

time: 122 us -> 38.1 us (0.31)
  other arithmetic: 44.4 us -> 0.08 us
  local copies, waits for them, and re-layouts: 26.5 us -> 0 us
  starting transfers between devices: 23.6 us -> 14.2 us
  Pallas kernels: 0 us -> 8.91 us
  waiting for transfers between devices: 20.6 us -> 14.8 us
  matrix products: 5.67 us -> 0 us
    scatter-add x4 -> x0, other arithmetic: 29.1 us -> none  [add_terms(): return summed.at[places].add(masked)]
    another operation x12 -> x0, local copies, waits for them, and re-layouts: 12.2 us -> none
    ppermute x20 -> x7, starting transfers between devices: 23.6 us -> 14.2 us  [the longest x4 11.2 us: along(): return lax.ppermute(block, 'row', route)]
    pallas_call x0 -> x3, Pallas kernels: none -> 8.91 us  [the longest x1 4.35 us: multiply_tiles(): pl.pallas_call(functools.partial(early_kernel, tiles, slots), out_shape=(...]
    gather x12 -> x0, local copies, waits for them, and re-layouts: 6.9 us -> none  [the longest x4 3.79 us: add_terms(): picked = right_vals[partner]]
    select_n x20 -> x0, other arithmetic: 6.53 us -> none  [the longest x2 1.84 us: skew_left(): jnp.where(selected, moved_vals, left_vals)]
    ppermute x20 -> x7, waiting for transfers between devices: 20.6 us -> 14.8 us  [the longest x4 9.17 us: along(): return lax.ppermute(block, 'row', route)]
    dot_general x4 -> x0, matrix products: 5.67 us -> none  [add_terms(): jnp.einsum('aij,awjk->awik', left_vals, picked, preferred_element_type=jn...]
  transfers between devices with their start and end apart: 20 -> 7, of which waited for: 3 -> 3; matrix products, arithmetic and copies ran while one was open for 43% -> 0% of each run, Pallas kernels for 0% -> 11%
where the time goes in v1:
time: 38.1 us
  waiting for transfers between devices  14.8 us (39%)
  starting transfers between devices  14.2 us (37%)
  Pallas kernels  8.91 us (23%)
    ppermute x4, starting transfers between devices, along(): return lax.ppermute(block, 'row', route)  11.2 us
    ppermute x4, waiting for transfers between devices, along(): return lax.ppermute(block, 'row', route)  9.17 us
    ppermute x1, waiting for transfers between devices, line_of_four(): left_x = lax.ppermute(left, CR, across)  5.6 us
    pallas_call x1, Pallas kernels, multiply_tiles(): pl.pallas_call(functools.partial(early_kernel, tiles, slots), out_shape=(...  4.35 us
    pallas_call x1, Pallas kernels, multiply_tiles(): pl.pallas_call(functools.partial(late_kernel, options, slots), out_shape=...  3.41 us
    ppermute x1, starting transfers between devices, line_of_four(): left_x = lax.ppermute(left, CR, across)  3 us
    pallas_call x1, Pallas kernels, pack(): pl.pallas_call(pack_kernel, out_shape=(packed, packed), in_specs=[HBM] *...  1.15 us
  transfers between devices with their start and end apart: 7, of which 3 were waited for; matrix products, arithmetic and copies ran while one was open for 0% of the time, Pallas kernels for 11%

profile of v1, /device:TPU:0, one launch (start us, length us, event | category | flops | bytes accessed | tf_op | source)
XLA Modules:
  0.0 38.1 jit_solution(4053399253309378336)
XLA Ops:
  0.0 1.1 %shard_map.46 = (bf16[1552,128]{1,0:T(8,128)(2,1)S(1)}, bf16[1552,128]{1,0:T(8,128)(2,1)S(1)}) custom-call(bf16[1536,128]{1,0:T(8,128)(2,1)} %bitcast.9, s32[2,12]{1,0:T(2,128)} %bitcast.11, bf16[1536,128]{1,0:T(8,128)(2,1)} %bitcast.10, s32[2,12]{1,0:T(2,128)} %bitcast.12), custom_call_target="tpu_custom_call" | custom-call | tf_op jit(solution)/shard_map/pallas_call | solution.py:44
  1.2 3.0 %collective-permute-start.1 = (bf16[1552,128]{1,0:T(8,128)(2,1)S(1)}, bf16[1552,128]{1,0:T(8,128)(2,1)S(1)}, u32[]{:S(2)}, u32[]{:S(2)}) collective-permute-start(bf16[1552,128]{1,0:T(8,128)(2,1)S(1)} %get-tuple-element.12.refs_0_), channel_id=1, source_target_pairs={{0,2},{1,3},{2,0},{3,1},{4,6},{5,7},{6,4},{7,5},{8,10},{9,11},{10,... | collective-permute-start | bytes 1191944 | tf_op jit(solution)/shard_map/ppermute | solution.py:278
  4.2 3.6 %collective-permute-start.3 = (bf16[1552,128]{1,0:T(8,128)(2,1)S(1)}, bf16[1552,128]{1,0:T(8,128)(2,1)S(1)}, u32[]{:S(2)}, u32[]{:S(2)}) collective-permute-start(bf16[1552,128]{1,0:T(8,128)(2,1)S(1)} %get-tuple-element.13.refs_4_), channel_id=1, source_target_pairs={{4,8},{8,4},{0,12},{12,0},{5,9},{9,5},{1,13},{13,1},{6,10},{10,6},... | collective-permute-start | bytes 1191944 | tf_op jit(solution)/shard_map/ppermute | solution.py:272
  7.8 0.0 collective-permute-start
  7.8 5.6 %collective-permute-done.1.refs_2_ = bf16[1552,128]{1,0:T(8,128)(2,1)S(1)} collective-permute-done((bf16[1552,128]{1,0:T(8,128)(2,1)S(1)}, bf16[1552,128]{1,0:T(8,128)(2,1)S(1)}, u32[]{:S(2)}, u32[]{:S(2)}) %collective-permute-start.1) | collective-permute-done | bytes 397344 | tf_op jit(solution)/shard_map/ppermute | solution.py:278
  13.4 0.0 collective-permute-start.2
  13.4 1.8 %collective-permute-start.6 = (bf16[1552,128]{1,0:T(8,128)(2,1)S(1)}, bf16[1552,128]{1,0:T(8,128)(2,1)S(1)}, u32[]{:S(2)}, u32[]{:S(2)}) collective-permute-start(bf16[1552,128]{1,0:T(8,128)(2,1)S(1)} %get-tuple-element.13.refs_4_), channel_id=1, source_target_pairs={{0,4},{4,0},{8,12},{12,8},{1,5},{5,1},{9,13},{13,9},{2,6},{6,2},{1... | collective-permute-start | bytes 1191944 | tf_op jit(solution)/shard_map/ppermute | solution.py:272
  15.2 4.5 %collective-permute-start.4 = (bf16[1552,128]{1,0:T(8,128)(2,1)S(1)}, bf16[1552,128]{1,0:T(8,128)(2,1)S(1)}, u32[]{:S(2)}, u32[]{:S(2)}) collective-permute-start(bf16[1552,128]{1,0:T(8,128)(2,1)S(1)} %get-tuple-element.13.refs_4_), channel_id=1, source_target_pairs={{0,8},{12,4},{1,9},{13,5},{2,10},{14,6},{3,11},{15,7},{16,24},{28,... | collective-permute-start | bytes 1191944 | tf_op jit(solution)/shard_map/ppermute | solution.py:272
  19.7 0.0 collective-permute-done.3.refs_5_
  19.7 1.3 %collective-permute-start.5 = (bf16[1552,128]{1,0:T(8,128)(2,1)S(1)}, bf16[1552,128]{1,0:T(8,128)(2,1)S(1)}, u32[]{:S(2)}, u32[]{:S(2)}) collective-permute-start(bf16[1552,128]{1,0:T(8,128)(2,1)S(1)} %collective-permute-done.3.refs_5_), channel_id=1, source_target_pairs={{4,0},{8,12},{5,1},{9,13},{6,2},{10,14},{7,3},{11,15},{20,16},{24,... | collective-permute-start | bytes 1191944 | tf_op jit(solution)/shard_map/ppermute | solution.py:272
  21.0 0.1 add_xor_fusion.links
  21.1 0.0 collective-permute-done.refs_1_
  21.1 0.0 collective-permute-done.2.refs_3_
  21.1 4.4 %shard_map.47 = (bf16[1024,1024]{1,0:T(8,128)(2,1)}, f32[8192,128]{1,0:T(8,128)S(1)}, bf16[6144,128]{1,0:T(8,128)(2,1)S(1)}, s32[32,128]{1,0:T(8,128)S(4)}) custom-call(s32[4]{0:T(128)S(1)} %add_xor_fusion.links, bf16[1552,128]{1,0:T(8,128)(2,1)S(1)} %get-tuple-element.12.refs_0_, bf16[1552,128]{1,0:T(8,128)(2,1)S(1)} %collective-permute-done.refs_1_, ...), custom_call_target="tpu_custom_call" | custom-call | tf_op jit(solution)/shard_map/pallas_call | solution.py:213
  25.5 0.0 collective-permute-done.6.refs_2_
  25.5 7.5 %collective-permute-done.4.refs_0_ = bf16[1552,128]{1,0:T(8,128)(2,1)S(1)} collective-permute-done((bf16[1552,128]{1,0:T(8,128)(2,1)S(1)}, bf16[1552,128]{1,0:T(8,128)(2,1)S(1)}, u32[]{:S(2)}, u32[]{:S(2)}) %collective-permute-start.4) | collective-permute-done | bytes 397344 | tf_op jit(solution)/shard_map/ppermute | solution.py:272
  33.0 1.6 %collective-permute-done.5.refs_1_ = bf16[1552,128]{1,0:T(8,128)(2,1)S(1)} collective-permute-done((bf16[1552,128]{1,0:T(8,128)(2,1)S(1)}, bf16[1552,128]{1,0:T(8,128)(2,1)S(1)}, u32[]{:S(2)}, u32[]{:S(2)}) %collective-permute-start.5) | collective-permute-done | bytes 397344 | tf_op jit(solution)/shard_map/ppermute | solution.py:272
  34.7 3.4 %shard_map.48 = (bf16[1024,1024]{1,0:T(8,128)(2,1)}, f32[8192,128]{1,0:T(8,128)S(1)}) custom-call(s32[4]{0:T(128)S(1)} %add_xor_fusion.links, s32[1]{0:T(128)} %bitcast.4.late, s32[32,128]{1,0:T(8,128)S(4)} %get-tuple-element.14.lc, bf16[6144,128]{1,0:T(8,128)(2,1)S(1)} %get-tuple-element.15.lall, ...), custom_call_target="tpu_custom_call", output_to_operand_aliasing={{1}: (4, {}), {0}: (8, {})} | custom-call | tf_op jit(solution)/shard_map/pallas_call | solution.py:235
Async XLA Ops:
  1.2 12.2 %collective-permute-start.1 = (bf16[1552,128]{1,0:T(8,128)(2,1)S(1)}, bf16[1552,128]{1,0:T(8,128)(2,1)S(1)}, u32[]{:S(2)}, u32[]{:S(2)}) collective-permute-start(bf16[1552,128]{1,0:T(8,128)(2,1)S(1)} %get-tuple-element.12.refs_0_), channel_id=1, source_target_pairs={{0,2},{1,3},{2,0},{3,1},{4,6},{5,7},{6,4},{7,5},{8,10},{9,11},{10,... | collective-permute-start | bytes 1191944 | tf_op jit(solution)/shard_map/ppermute | solution.py:278
  4.2 15.5 %collective-permute-start.3 = (bf16[1552,128]{1,0:T(8,128)(2,1)S(1)}, bf16[1552,128]{1,0:T(8,128)(2,1)S(1)}, u32[]{:S(2)}, u32[]{:S(2)}) collective-permute-start(bf16[1552,128]{1,0:T(8,128)(2,1)S(1)} %get-tuple-element.13.refs_4_), channel_id=1, source_target_pairs={{4,8},{8,4},{0,12},{12,0},{5,9},{9,5},{1,13},{13,1},{6,10},{10,6},... | collective-permute-start | bytes 1191944 | tf_op jit(solution)/shard_map/ppermute | solution.py:272
  7.8 13.4 %collective-permute-start = (bf16[1552,128]{1,0:T(8,128)(2,1)S(1)}, bf16[1552,128]{1,0:T(8,128)(2,1)S(1)}, u32[]{:S(2)}, u32[]{:S(2)}) collective-permute-start(bf16[1552,128]{1,0:T(8,128)(2,1)S(1)} %get-tuple-element.12.refs_0_), channel_id=1, source_target_pairs={{0,1},{1,0},{2,3},{3,2},{4,5},{5,4},{6,7},{7,6},{8,9},{9,8},{10,11... | collective-permute-start | bytes 1191944 | tf_op jit(solution)/shard_map/ppermute | solution.py:279
  13.4 7.8 %collective-permute-start.2 = (bf16[1552,128]{1,0:T(8,128)(2,1)S(1)}, bf16[1552,128]{1,0:T(8,128)(2,1)}, u32[]{:S(2)}, u32[]{:S(2)}) collective-permute-start(bf16[1552,128]{1,0:T(8,128)(2,1)S(1)} %collective-permute-done.1.refs_2_), channel_id=1, source_target_pairs={{0,1},{1,0},{2,3},{3,2},{4,5},{5,4},{6,7},{7,6},{8,9},{9,8},{10,11... | collective-permute-start | bytes 1191944 | tf_op jit(solution)/shard_map/ppermute | solution.py:280
  13.4 12.1 %collective-permute-start.6 = (bf16[1552,128]{1,0:T(8,128)(2,1)S(1)}, bf16[1552,128]{1,0:T(8,128)(2,1)S(1)}, u32[]{:S(2)}, u32[]{:S(2)}) collective-permute-start(bf16[1552,128]{1,0:T(8,128)(2,1)S(1)} %get-tuple-element.13.refs_4_), channel_id=1, source_target_pairs={{0,4},{4,0},{8,12},{12,8},{1,5},{5,1},{9,13},{13,9},{2,6},{6,2},{1... | collective-permute-start | bytes 1191944 | tf_op jit(solution)/shard_map/ppermute | solution.py:272
  15.2 17.8 %collective-permute-start.4 = (bf16[1552,128]{1,0:T(8,128)(2,1)S(1)}, bf16[1552,128]{1,0:T(8,128)(2,1)S(1)}, u32[]{:S(2)}, u32[]{:S(2)}) collective-permute-start(bf16[1552,128]{1,0:T(8,128)(2,1)S(1)} %get-tuple-element.13.refs_4_), channel_id=1, source_target_pairs={{0,8},{12,4},{1,9},{13,5},{2,10},{14,6},{3,11},{15,7},{16,24},{28,... | collective-permute-start | bytes 1191944 | tf_op jit(solution)/shard_map/ppermute | solution.py:272
  19.7 14.9 %collective-permute-start.5 = (bf16[1552,128]{1,0:T(8,128)(2,1)S(1)}, bf16[1552,128]{1,0:T(8,128)(2,1)S(1)}, u32[]{:S(2)}, u32[]{:S(2)}) collective-permute-start(bf16[1552,128]{1,0:T(8,128)(2,1)S(1)} %collective-permute-done.3.refs_5_), channel_id=1, source_target_pairs={{4,0},{8,12},{5,1},{9,13},{6,2},{10,14},{7,3},{11,15},{20,16},{24,... | collective-permute-start | bytes 1191944 | tf_op jit(solution)/shard_map/ppermute | solution.py:272
